TPU v7x, 32 devices: a whole 2x2x4 slice. The times are simulated.
32 devices in a mesh: grp: 2 (over y), orient: 4 (over z), frame: 4 (over x, core).
Axes of the slice: x: 2, y: 2, z: 4, core: 2. Of those that a mesh axis runs over, the one named last changes fastest.
Arguments:
- photons: int32 [1024, 65536], P(('grp', 'frame'), 'orient'), parts along dimension 0, may hold values from 0 to 7
- masses: int32 [1024, 16, 8], P(('grp', 'frame'), 'orient'), parts along dimension 0, may hold values from 1 to 4097, as said below
- maps: int32 [16, 512], P('orient'), may hold values from 0 to 511
- model: float32 [131072], P('grp'), parts along dimension 0, may hold values from 0.2 to 5
- fluence: float32 [1024], P(('grp', 'frame')), parts along dimension 0, may hold values from 0.3 to 3
- level_scale: float32 [8], replicated, may hold values from 0.25 to 4
Outputs:
- gain: float32 [131072], P(('grp', 'orient')), parts along dimension 0
- new_fluence: float32 [1024], P(('grp', 'frame')), parts along dimension 0
There are 2 independent parts, one for each index of `grp`. A program takes and returns all parts, laid end to end along the dimension named above; an argument that names none is the same for every part. Nothing has to cross between parts.
Inputs may be any that keep to these rules, and one draw needn't show every extreme that they name: Positive fixed-point posterior masses.
All inputs are finite; a program needn't handle non-finite values.
Results may differ from a plain program's by a relative error of at most 0.00011.
Values sent between devices are 32-bit elements; how exact they have to be, the bound alone decides.
A program may use at most 64 MiB of HBM per device.

v0:
```python
import jax
import jax.numpy as jnp
from jax import lax
from jax.sharding import PartitionSpec as P

PIX = 65536
BLOCK = 128
ITERS = 2


def on_device(photons, masses, maps, model, fluence, level_scale):
    mass = masses.astype(jnp.float32)
    frame_part = jnp.sum(mass, axis=(1, 2))
    photon_rows = jnp.sum(photons, axis=1).astype(jnp.float32)
    total, frame_photons = lax.psum((frame_part, photon_rows), "orient")
    prob = mass / total[:, None, None]
    tilted = jnp.sum(prob * level_scale[None, None, :], axis=2)
    column_part = jnp.sum(photons, axis=0).astype(jnp.float32)
    pixel_photons = lax.psum(column_part, "frame")
    table = model.reshape(PIX // BLOCK, BLOCK)
    local_orient = maps.shape[0]
    slices = table[maps].reshape(local_orient, PIX)
    columns = lax.all_to_all(slices, "orient", split_axis=1, concat_axis=0, tiled=True)
    first_orient = lax.axis_index("orient") * local_orient
    phi = fluence
    gain_own = pixel_photons
    for step in range(ITERS):
        weight = lax.psum(jnp.dot(phi, tilted, precision=lax.Precision.HIGHEST), "frame")
        weight_all = lax.all_gather(weight, "orient", axis=0, tiled=True)
        expected = jnp.dot(weight_all, columns, precision=lax.Precision.HIGHEST)
        gain_own = pixel_photons / expected
        seen_all = lax.psum(jnp.dot(columns, gain_own, precision=lax.Precision.HIGHEST), "orient")
        seen = lax.dynamic_slice_in_dim(seen_all, first_orient, local_orient, 0)
        fluence_part = jnp.dot(tilted, seen, precision=lax.Precision.HIGHEST)
        phi = frame_photons / lax.psum(fluence_part, "orient")
    return (gain_own, phi)


def solution(mesh):
    placed = (
        P(("grp", "frame"), "orient"),
        P(("grp", "frame"), "orient", None),
        P("orient", None),
        P("grp"),
        P(("grp", "frame")),
        P(),
    )
    return jax.shard_map(
        on_device,
        mesh=mesh,
        in_specs=placed,
        out_specs=(P(("grp", "orient")), P(("grp", "frame"))),
        check_vma=False,
    )
```

profile of v0, /device:TPU:0, one launch (start us, length us, event | category | flops | bytes accessed | tf_op | source)
XLA Modules:
  0.0 148.9 jit_solution(16945898156851092513)
XLA Ops:
  7.2 0.7 fusion
  7.9 0.2 copy-done
  8.1 5.5 %gather_fusion = f32[2048,128]{1,0:T(8,128)S(1)} fusion(f32[512,128]{1,0:T(8,128)S(1)} %bitcast.50, s32[2048]{0:T(1024)S(1)} %broadcast_clamp_fusion), kind=kCustom, calls=%fused_computation | custom fusion | bytes 2105344 | tf_op jit(solution)/shard_map/gather | solution.py:22
  13.6 0.4 all_to_all.14
  14.1 1.7 %copy.9 = f32[4,4,16384]{2,0,1:T(4,128)} copy(f32[4,4,16384]{2,1,0:T(4,128)S(1)} %all_to_all.14) | data formatting | bytes 2097152 | tf_op jit(solution)/shard_map/all_to_all | solution.py:23
  15.8 6.3 %all-to-all-start = ((f32[4,4,16384]{2,0,1:T(4,128)}), f32[4,4,16384]{2,0,1:T(4,128)S(1)}, u32[]{:S(2)}, u32[]{:S(2)}) async-start(f32[4,4,16384]{2,0,1:T(4,128)} %copy.9), calls=%async_computation | async-start | bytes 2097152 | tf_op jit(solution)/shard_map/all_to_all | solution.py:23
  22.1 4.1 %fusion.12 = (s32[128]{0:T(128)S(1)}, s32[16384]{0:T(1024)S(1)}) fusion(s32[128,16384]{1,0:T(8,128)} %param.6), kind=kLoop, calls=%fused_computation.23 | loop fusion | flops 4177792 | bytes 8454656 | tf_op jit(solution)/shard_map/reduce_sum | solution.py:14
  26.2 0.6 convert_element_type.9
  26.9 18.4 %psum.65 = f32[128]{0:T(128)S(1)} all-reduce(f32[128]{0:T(128)S(1)} %convert_reduce_fusion), channel_id=1, replica_groups=mesh['grp'=2,'orient'=4,'frame'=4] {'orient'}, use_global_device_ids=true, to_apply=%region_5.0 | all-reduce | flops 128 | bytes 1024 | tf_op jit(solution)/shard_map/psum | solution.py:15
  45.4 0.1 convolution_bitcast_fusion.5
  45.5 5.7 %psum.66 = f32[4]{0:T(128)S(1)} all-reduce(f32[4]{0:T(128)S(1)} %convolution_bitcast_fusion.5), channel_id=1, replica_groups=mesh['grp'=2,'orient'=4,'frame'=4] {'frame'}, use_global_device_ids=true, to_apply=%region_7.0 | all-reduce | flops 4 | bytes 32 | tf_op jit(solution)/shard_map/psum | solution.py:28
  51.2 0.6 dynamic-slice
  52.5 0.2 dynamic-update-slice
  52.7 14.6 %all-reduce = f32[16]{0:T(128)S(1)} all-reduce(f32[16]{0:T(128)S(1)} %dynamic-update-slice), channel_id=1, replica_groups=mesh['grp'=2,'orient'=4,'frame'=4] {'orient'}, use_global_device_ids=true, to_apply=%add | all-reduce | flops 16 | bytes 128
  67.4 0.4 all_to_all.17
  67.7 0.6 fusion.6
  68.3 12.5 %all-reduce.5.cloned.1.call-done = f32[16384]{0:T(1024)} async-done(((f32[16384]{0:T(1024)}), f32[16384]{0:T(1024)}) %all-reduce.5.cloned.1.call-update) | async-done | bytes 65552 | tf_op jit(solution)/shard_map/psum | solution.py:19
  80.8 0.9 div.22
  81.7 1.3 convolution_bitcast_fusion.1
  83.0 11.7 %psum.67 = f32[16]{0:T(128)S(1)} all-reduce(f32[16]{0:T(128)S(1)} %convolution_bitcast_fusion.1), channel_id=1, replica_groups=mesh['grp'=2,'orient'=4,'frame'=4] {'orient'}, use_global_device_ids=true, to_apply=%region_8.0 | all-reduce | flops 16 | bytes 128 | tf_op jit(solution)/shard_map/psum | solution.py:32
  94.7 0.2 convolution_bitcast_fusion.4
  94.9 8.4 %all-reduce.2 = (f32[128]{0:T(128)S(1)}, f32[128]{0:T(128)S(1)}) all-reduce(f32[128]{0:T(128)S(1)} %convert_element_type.10, f32[128]{0:T(128)S(1)} %convolution_bitcast_fusion.4), channel_id=1, replica_groups=mesh['grp'=2,'orient'=4,'frame'=4] {'orient'}, use_global_device_ids=true, to_apply=%region_3.0 | all-reduce | flops 256 | bytes 2048 | tf_op jit(solution)/shard_map/psum | solution.py:15
  103.4 5.9 %psum.69 = f32[4]{0:T(128)S(1)} all-reduce(f32[4]{0:T(128)S(1)} %convolution_bitcast_fusion.3), channel_id=1, replica_groups=mesh['grp'=2,'orient'=4,'frame'=4] {'frame'}, use_global_device_ids=true, to_apply=%region_10.0 | all-reduce | flops 4 | bytes 32 | tf_op jit(solution)/shard_map/psum | solution.py:28
  109.2 0.2 dynamic-update-slice.1
  109.5 10.3 %all-reduce.1 = f32[16]{0:T(128)S(1)} all-reduce(f32[16]{0:T(128)S(1)} %dynamic-update-slice.1), channel_id=1, replica_groups=mesh['grp'=2,'orient'=4,'frame'=4] {'orient'}, use_global_device_ids=true, to_apply=%add.1 | all-reduce | flops 16 | bytes 128
  119.8 0.6 fusion.2
  120.4 0.9 div.24
  121.3 1.3 convolution_bitcast_fusion
  122.7 8.4 %psum.70 = f32[16]{0:T(128)S(1)} all-reduce(f32[16]{0:T(128)S(1)} %convolution_bitcast_fusion), channel_id=1, replica_groups=mesh['grp'=2,'orient'=4,'frame'=4] {'orient'}, use_global_device_ids=true, to_apply=%region_11.0 | all-reduce | flops 16 | bytes 128 | tf_op jit(solution)/shard_map/psum | solution.py:32
  131.0 0.2 convolution_bitcast_fusion.2
  131.2 10.4 %psum.71 = f32[128]{0:T(128)S(1)} all-reduce(f32[128]{0:T(128)S(1)} %convolution_bitcast_fusion.2), channel_id=1, replica_groups=mesh['grp'=2,'orient'=4,'frame'=4] {'orient'}, use_global_device_ids=true, to_apply=%region_12.0 | all-reduce | flops 128 | bytes 1024 | tf_op jit(solution)/shard_map/psum | solution.py:35
  141.6 0.5 div.25
  (22 shorter events, 0.3 us)
Async XLA Ops:
  7.2 1.0 copy-start
  13.6 13.2 %copy-start.2 = (s32[128,4,8]{0,2,1:T(8,128)S(1)}, s32[128,4,8]{0,2,1:T(8,128)}, u32[]{:S(2)}) copy-start(s32[128,4,8]{0,2,1:T(8,128)} %param.7) | copy-start | bytes 49156
  13.6 31.7 %copy-start.3 = (f32[8]{0:T(128)S(1)}, f32[8]{0:T(128)}, u32[]{:S(2)}) copy-start(f32[8]{0:T(128)} %param.11) | copy-start | bytes 100
  13.6 31.8 %copy-start.4 = (f32[128]{0:T(128)S(1)}, f32[128]{0:T(128)}, u32[]{:S(2)}) copy-start(f32[128]{0:T(128)} %param.10) | copy-start | bytes 1540
  13.6 37.6 %copy-start.5 = (u32[32]{0:T(128)S(1)}, u32[32]{0:T(128)}, u32[]{:S(2)}) copy-start(u32[32]{0:T(128)} %constant.18) | copy-start | bytes 388
  15.8 51.6 %all-to-all-start = ((f32[4,4,16384]{2,0,1:T(4,128)}), f32[4,4,16384]{2,0,1:T(4,128)S(1)}, u32[]{:S(2)}, u32[]{:S(2)}) async-start(f32[4,4,16384]{2,0,1:T(4,128)} %copy.9), calls=%async_computation | async-start | bytes 2097152 | tf_op jit(solution)/shard_map/all_to_all | solution.py:23
  22.1 58.7 %all-reduce.5.cloned.1.call-start = ((), (), s32[]{:S(2)}) async-start(), calls=%async_computation.1 | async-start | bytes 131072 | tf_op jit(solution)/shard_map/psum | solution.py:19
  121.3 20.8 %copy-start.1 = (f32[16384]{0:T(1024)}, f32[16384]{0:T(1024)S(1)}, u32[]{:S(2)}) copy-start(f32[16384]{0:T(1024)S(1)} %div.24) | copy-start | bytes 196612
Sparse Core Ops, SparseCore 0:
  45.7 35.0 all-reduce.4
where the time goes:
time: 149 us
  blocking collectives  93.7 us (63%)
  between operations  14.8 us (10%)
  waiting for transfers between devices  12.5 us (8%)
  local copies, waits for them, and re-layouts  9.22 us (6%)
  other arithmetic  7.85 us (5%)
  starting transfers between devices  6.32 us (4%)
  matrix products  4.59 us (3%)
    psum x2, blocking collectives, on_device(): total, frame_photons = lax.psum((frame_part, photon_rows), 'orient')  26.8 us
    unnamed x2, blocking collectives  25 us
    psum x2, blocking collectives, on_device(): lax.psum(jnp.dot(columns, gain_own, precision=lax.Precision.HIGHEST), 'or...  20 us
    psum x1, waiting for transfers between devices, on_device(): pixel_photons = lax.psum(column_part, 'frame')  12.5 us
    psum x2, blocking collectives, on_device(): lax.psum(jnp.dot(phi, tilted, precision=lax.Precision.HIGHEST), 'frame')  11.5 us
    psum x1, blocking collectives, on_device(): phi = frame_photons / lax.psum(fluence_part, 'orient')  10.4 us
    all_to_all x1, starting transfers between devices, on_device(): lax.all_to_all(slices, 'orient', split_axis=1, concat_axis=0, tiled=True)  6.32 us
    gather x1, local copies, waits for them, and re-layouts, on_device(): slices = table[maps].reshape(local_orient, PIX)  5.46 us
  transfers between devices with their start and end apart: 2, of which 1 were waited for; matrix products, arithmetic and copies ran while one was open for 4% of the time, Pallas kernels for 0%

commit v1 on v0

v1 whole, which is shorter than its diff:
```python
import functools
import jax
import jax.numpy as jnp
from jax import lax
from jax.experimental import pallas as pl
from jax.experimental.pallas import tpu as pltpu
from jax.sharding import PartitionSpec as P

BLOCK = 128
ITERS = 2
MESH = pl.DeviceIdType.MESH


def emc_kernel(
    O, F, OL, L, D, MB, NB, CH,
    photons, masses, maps, model, fluence, scale,
    gain_out, phi_out,
    ph, mass_v, flu_v, scale_v, table, map_v, map_s, sl,
    stat, til, cols, parts, note, note_in, gain_v, phi_v,
    ph_sem, in_sem, map_sem, loc_sem, stat_sem, col_sem, note_sem, gain_sem,
):
    N = O * F
    R = O * OL
    o = lax.axis_index("orient")
    f = lax.axis_index("frame")
    me = o * F + f
    width = NB * BLOCK
    piece = width // CH

    def spot(t):
        n = lax.rem(me + t, N)
        return lax.div(n, F), lax.rem(n, F)

    def others(body):
        if N <= 16:
            for t in range(1, N):
                body(t)
        else:
            def step(t, c):
                body(t)
                return c
            lax.fori_loop(1, N, step, 0)

    order = [(F // 2 + i) % F for i in range(F)]
    order = [i for i in order if i != 0] + [0]

    small = [
        pltpu.make_async_copy(masses, mass_v, in_sem.at[0]),
        pltpu.make_async_copy(scale, scale_v, in_sem.at[1]),
        pltpu.make_async_copy(fluence, flu_v, in_sem.at[2]),
        pltpu.make_async_copy(model, table, in_sem.at[3]),
    ]
    first = me * NB
    for c in small:
        c.start()
    own_map = pltpu.make_async_copy(
        maps.at[:, pl.ds(pl.multiple_of(lax.div(first, 128) * 128, 128), 128)], map_v.at[o], in_sem.at[4])
    own_map.start()

    def read(i, c):
        g = lax.rem(f + order[i], F)
        start = pl.multiple_of(g * width + c * piece, 128)
        return pltpu.make_async_copy(
            photons.at[:, pl.ds(start, piece)], ph.at[i, c], ph_sem.at[i, c])

    for i in range(F):
        for c in range(CH):
            read(i, c).start()

    barrier = pltpu.get_barrier_semaphore()

    def greet(t):
        a, b = spot(t)
        pl.semaphore_signal(barrier, inc=1, device_id={"orient": a, "frame": b}, device_id_type=MESH)
    others(greet)

    for c in small[:3]:
        c.wait()
    m = mass_v[...].astype(jnp.float32)
    eye = lax.broadcasted_iota(jnp.int32, (L, L), 0) == lax.broadcasted_iota(jnp.int32, (L, L), 1)
    sc = jnp.sum(jnp.where(eye, jnp.broadcast_to(scale_v[...], (L, L)), 0.0), axis=1, keepdims=True)
    tot = jnp.zeros((1, D), jnp.float32)
    for k in range(OL):
        stat[me, k:k + 1, :] = jnp.sum(m[k] * sc, axis=0, keepdims=True)
        tot += jnp.sum(m[k], axis=0, keepdims=True)
    stat[me, OL:OL + 1, :] = tot
    stat[me, OL + 1:OL + 2, :] = flu_v[...]

    pl.semaphore_wait(barrier, N - 1)

    def send_map(t):
        a = lax.rem(o + t, O)
        block = lax.div((a * F + f) * NB, 128)
        return pltpu.make_async_remote_copy(
            src_ref=maps.at[:, pl.ds(pl.multiple_of(block * 128, 128), 128)],
            dst_ref=map_v.at[o], send_sem=map_sem.at[0], recv_sem=map_sem.at[1],
            device_id={"orient": a}, device_id_type=MESH)
    for t in range(1, O):
        send_map(t).start()

    def send_stat(t):
        a, b = spot(t)
        pltpu.make_async_remote_copy(
            src_ref=stat.at[me], dst_ref=stat.at[me], send_sem=stat_sem.at[0], recv_sem=stat_sem.at[1],
            device_id={"orient": a, "frame": b}, device_id_type=MESH).start()
    others(send_stat)

    def sums(i, rows):
        for c in range(CH):
            read(i, c).wait()

            def tile(q, acc):
                x = ph[i, c, :, pl.ds(pl.multiple_of(q * 128, 128), 128)]
                cols[i, pl.ds(c * (piece // 128) + q, 1), :] = jnp.sum(x, axis=0, keepdims=True).astype(jnp.float32)
                return acc + x
            rows = lax.fori_loop(0, piece // 128, tile, rows, unroll=2)
        return rows

    def send_cols(i):
        pltpu.make_async_remote_copy(
            src_ref=cols.at[i], dst_ref=parts.at[f], send_sem=col_sem.at[0], recv_sem=col_sem.at[1],
            device_id={"frame": lax.rem(f + order[i], F)}, device_id_type=MESH).start()

    def all_of(ref, sem, count):
        c = pltpu.make_async_remote_copy(
            src_ref=ref.at[pl.ds(0, count)], dst_ref=ref.at[pl.ds(0, count)],
            send_sem=sem.at[0], recv_sem=sem.at[1],
            device_id={"orient": lax.rem(o + 1, O)}, device_id_type=MESH)
        return c

    rows = jnp.zeros((D, 128), jnp.int32)
    half = F // 2
    for i in range(half):
        rows = sums(i, rows)
        send_cols(i)

    own_map.wait()
    maps_in = all_of(map_v, map_sem, O - 1)
    maps_in.wait_recv()
    to_s = pltpu.make_async_copy(map_v, map_s, loc_sem.at[0])
    to_s.start()
    small[3].wait()

    stats_in = all_of(stat, stat_sem, N - 1)
    stats_in.wait_recv()
    for g in range(F):
        t = stat[g, OL:OL + 1, :]
        for a in range(1, O):
            t += stat[a * F + g, OL:OL + 1, :]
        inv = 1.0 / t
        for a in range(O):
            til[g, a * OL:(a + 1) * OL, :] = stat[a * F + g, 0:OL, :] * inv

    to_s.wait()
    base = lax.rem(first, 128)

    def look(r, carry):
        a, k = lax.div(r, OL), lax.rem(r, OL)
        for b in range(NB):
            sl[r, b:b + 1, :] = table[pl.ds(map_s[a, k, base + b], 1), :]
        return carry
    lax.fori_loop(0, R, look, 0)

    def expected_of(phis):
        w = til[0] * phis[0]
        for g in range(1, F):
            w += til[g] * phis[g]
        w = jnp.broadcast_to(jnp.sum(w, axis=1, keepdims=True), (R, BLOCK))
        e = sl[0] * w[0:1, :]
        for r in range(1, R):
            e += sl[r] * w[r:r + 1, :]
        return e

    expected = expected_of([stat[g, OL + 1:OL + 2, :] for g in range(F)])

    for i in range(half, F):
        rows = sums(i, rows)
        if i < F - 1:
            send_cols(i)

    note[0, 1:2, :] = jnp.sum(rows.astype(jnp.float32).T, axis=0, keepdims=True)
    parts[f] = cols[F - 1]
    parts_in = all_of(parts, col_sem, F - 1)
    parts_in.wait_recv()
    pixel = parts[0]
    for g in range(1, F):
        pixel += parts[g]

    diag = lax.broadcasted_iota(jnp.int32, (R, 128), 0) == lax.broadcasted_iota(jnp.int32, (R, 128), 1)

    for step in range(ITERS):
        gain = pixel / expected
        if step == ITERS - 1:
            gain_v[f] = gain

            for t in range(1, F):
                pltpu.make_async_remote_copy(
                    src_ref=gain_v.at[f], dst_ref=gain_v.at[f], send_sem=gain_sem.at[0], recv_sem=gain_sem.at[1],
                    device_id={"frame": lax.rem(f + t, F)}, device_id_type=MESH).start()
        part = [jnp.sum(sl[r] * gain, axis=0, keepdims=True) for r in range(R)]
        part = jnp.sum(jnp.concatenate(part, axis=0), axis=1, keepdims=True)
        row = jnp.sum(jnp.where(diag, part, 0.0), axis=0, keepdims=True)
        note[step, 0:1, :] = row
        if step > 0:
            note[step, 1:2, :] = jnp.zeros((1, 128), jnp.float32)
        note_in[step, me] = note[step]

        def send_note(t):
            a, b = spot(t)
            pltpu.make_async_remote_copy(
                src_ref=note.at[step], dst_ref=note_in.at[step, me],
                send_sem=note_sem.at[step, 0], recv_sem=note_sem.at[step, 1],
                device_id={"orient": a, "frame": b}, device_id_type=MESH).start()
        others(send_note)
        notes = all_of(note_in.at[step], note_sem.at[step], N - 1)
        notes.wait_recv()
        seen = note_in[step, 0, 0:1, :]
        for n in range(1, N):
            seen += note_in[step, n, 0:1, :]
        seen = jnp.sum(jnp.where(diag, seen, 0.0), axis=1, keepdims=True)

        def photons_of(g):
            t = note_in[0, g, 1:2, :]
            for a in range(1, O):
                t += note_in[0, a * F + g, 1:2, :]
            return t
        if step < ITERS - 1:
            phis = [photons_of(g) / jnp.sum(til[g] * seen, axis=0, keepdims=True) for g in range(F)]
            expected = expected_of(phis)
        else:
            phi_v[...] = photons_of(f) / jnp.sum(til[f] * seen, axis=0, keepdims=True)
        notes.wait_send()

    phi_write = pltpu.make_async_copy(phi_v, phi_out, loc_sem.at[1])
    phi_write.start()
    gains = all_of(gain_v, gain_sem, F - 1)
    gains.wait_recv()
    gain_write = pltpu.make_async_copy(gain_v, gain_out, loc_sem.at[2])
    gain_write.start()
    maps_in.wait_send()
    stats_in.wait_send()
    parts_in.wait_send()
    gains.wait_send()
    phi_write.wait()
    gain_write.wait()


def on_device(O, F, photons, masses, maps, model, fluence, level_scale):
    D, OL, L = masses.shape
    wide = photons.shape[1]
    MB = maps.shape[1]
    N = O * F
    NB = wide // F // BLOCK
    CH = 2 if NB % 2 == 0 else 1
    R = O * OL
    f32, i32 = jnp.float32, jnp.int32
    V = pltpu.VMEM
    dma = pltpu.SemaphoreType.DMA
    SR = -(-(OL + 2) // 8) * 8
    body = functools.partial(emc_kernel, O, F, OL, L, D, MB, NB, CH)
    hbm = pl.BlockSpec(memory_space=pltpu.HBM)
    gain, phi = pl.pallas_call(
        body,
        out_shape=(jax.ShapeDtypeStruct((F, NB, BLOCK), f32), jax.ShapeDtypeStruct((1, D), f32)),
        in_specs=[hbm] * 6,
        out_specs=(hbm, hbm),
        scratch_shapes=[
            V((F, CH, D, NB * BLOCK // CH), i32),
            V((OL, L, D), i32), V((1, D), f32), V((1, L), f32),
            V((MB, BLOCK), f32), V((O, OL, 128), i32), pltpu.SMEM((O, OL, 128), i32),
            V((R, NB, BLOCK), f32), V((N, SR, D), f32), V((F, R, D), f32),
            V((F, NB, BLOCK), f32), V((F, NB, BLOCK), f32),
            V((ITERS, 2, 128), f32), V((ITERS, N, 2, 128), f32),
            V((F, NB, BLOCK), f32), V((1, D), f32),
            dma((F, CH)), dma((5,)), dma((2,)), dma((3,)), dma((2,)), dma((2,)), dma((ITERS, 2)), dma((2,)),
        ],
        compiler_params=pltpu.CompilerParams(
            collective_id=0, has_side_effects=True, vmem_limit_bytes=40 * 1024 * 1024),
    )(photons, jnp.transpose(masses, (1, 2, 0)), maps, model.reshape(MB, BLOCK),
      fluence.reshape(1, D), level_scale.reshape(1, L))
    return gain.reshape(-1), phi.reshape(-1)


def solution(mesh):
    placed = (
        P(("grp", "frame"), "orient"),
        P(("grp", "frame"), "orient", None),
        P("orient", None),
        P("grp"),
        P(("grp", "frame")),
        P(),
    )
    O, F = mesh.shape["orient"], mesh.shape["frame"]

    def run(*args):
        return on_device(O, F, *args)

    return jax.shard_map(
        run,
        mesh=mesh,
        in_specs=placed,
        out_specs=(P(("grp", "orient")), P(("grp", "frame"))),
        check_vma=False,
    )
```

time: 149 us -> 32.1 us (0.22)
  blocking collectives: 93.7 us -> 0 us
  Pallas kernels: 0 us -> 23 us
  between operations: 14.8 us -> 0.65 us
  waiting for transfers between devices: 12.5 us -> 0 us
  other arithmetic: 7.85 us -> 0 us
  starting transfers between devices: 6.32 us -> 0 us
  matrix products: 4.59 us -> 0 us
    psum x7 -> x0, blocking collectives: 68.7 us -> none  [the longest x2 26.8 us: on_device(): total, frame_photons = lax.psum((frame_part, photon_rows), 'orient')]
    unnamed x2 -> x0, blocking collectives: 25 us -> none
    pallas_call x0 -> x1, Pallas kernels: none -> 23 us  [on_device(): pl.pallas_call(body, out_shape=(jax.ShapeDtypeStruct((F, NB, BLOCK), f32)...]
    psum x1 -> x0, waiting for transfers between devices: 12.5 us -> none  [on_device(): pixel_photons = lax.psum(column_part, 'frame')]
    unnamed x18 -> x14, local copies, waits for them, and re-layouts: 1.3 us -> 8.19 us
    all_to_all x1 -> x0, starting transfers between devices: 6.32 us -> none  [on_device(): lax.all_to_all(slices, 'orient', split_axis=1, concat_axis=0, tiled=True)]
    gather x1 -> x0, local copies, waits for them, and re-layouts: 5.46 us -> none  [on_device(): slices = table[maps].reshape(local_orient, PIX)]
    dot_general x8 -> x0, matrix products: 4.59 us -> none  [the longest x2 2.69 us: on_device(): jnp.dot(columns, gain_own, precision=lax.Precision.HIGHEST)]
  transfers between devices with their start and end apart: 2 -> 0, of which waited for: 1 -> 0; matrix products, arithmetic and copies ran while one was open for 4% -> 0% of each run, Pallas kernels for 0% -> 0%
where the time goes in v1:
time: 32.1 us; the launch traced here: 31.8 us
  Pallas kernels  23 us (72%)
  local copies, waits for them, and re-layouts  8.19 us (26%)
  between operations  0.65 us (2%)
    pallas_call x1, Pallas kernels, on_device(): pl.pallas_call(body, out_shape=(jax.ShapeDtypeStruct((F, NB, BLOCK), f32)...  23 us
    unnamed x14, local copies, waits for them, and re-layouts  8.19 us

profile of v1, /device:TPU:0, one launch (start us, length us, event | category | flops | bytes accessed | tf_op | source)
XLA Modules:
  0.0 31.8 jit_solution(5147580659757610099)
XLA Ops:
  0.6 0.0 copy-start
  0.6 3.4 %copy-done = s32[128,16384]{1,0:T(8,128)S(1)} copy-done((s32[128,16384]{1,0:T(8,128)S(1)}, s32[128,16384]{1,0:T(8,128)}, u32[]{:S(2)}) %copy-start) | copy-done | bytes 8388632
  4.0 0.0 copy-start.1
  4.0 0.9 %copy-done.1 = f32[65536]{0:T(1024)S(1)} copy-done((f32[65536]{0:T(1024)S(1)}, f32[65536]{0:T(1024)}, u32[]{:S(2)}) %copy-start.1) | copy-done | bytes 262168
  5.0 0.0 copy-start.2
  5.0 0.7 %copy-done.2 = s32[128,4,8]{0,2,1:T(8,128)S(1)} copy-done((s32[128,4,8]{0,2,1:T(8,128)S(1)}, s32[128,4,8]{0,2,1:T(8,128)}, u32[]{:S(2)}) %copy-start.2) | copy-done | bytes 16408
  5.7 0.0 copy-start.3
  5.7 0.7 %copy-done.3 = s32[4,512]{1,0:T(4,128)S(1)} copy-done((s32[4,512]{1,0:T(4,128)S(1)}, s32[4,512]{1,0:T(4,128)}, u32[]{:S(2)}) %copy-start.3) | copy-done | bytes 8216
  6.4 0.0 copy-start.4
  6.4 0.7 %copy-done.4 = f32[128]{0:T(128)S(1)} copy-done((f32[128]{0:T(128)S(1)}, f32[128]{0:T(128)}, u32[]{:S(2)}) %copy-start.4) | copy-done | bytes 536
  7.0 0.0 copy-start.5
  7.0 0.7 %copy-done.5 = f32[8]{0:T(128)S(1)} copy-done((f32[8]{0:T(128)S(1)}, f32[8]{0:T(128)}, u32[]{:S(2)}) %copy-start.5) | copy-done | bytes 56
  7.7 23.0 %shard_map.77 = (f32[4,32,128]{2,1,0:T(8,128)S(1)}, f32[1,128]{1,0:T(1,128)S(1)}) custom-call(s32[128,16384]{1,0:T(8,128)S(1)} %copy-done, s32[4,8,128]{2,1,0:T(8,128)S(1)} %bitcast.8, s32[4,512]{1,0:T(4,128)S(1)} %copy-done.3, f32[512,128]{1,0:T(8,128)S(1)} %bitcast.6, f32[1,128]{1,0:T(1,128)S(1)} %bitcast.9, f32[1,8]{1,0:T(1,128)S(1)} %bitcast.10), custom_call_target="tpu_custom_call" | custom-call | tf_op jit(solution)/shard_map/pallas_call | solution.py:262
  30.7 0.6 %copy.10 = f32[16384]{0:T(1024)} copy(f32[16384]{0:T(1024)S(1)} %bitcast.7) | data formatting | bytes 131072
  31.3 0.5 %copy.11 = f32[128]{0:T(128)} copy(f32[128]{0:T(128)S(1)} %bitcast.11) | data formatting | bytes 1024
Async XLA Ops:
  0.6 3.4 %copy-start = (s32[128,16384]{1,0:T(8,128)S(1)}, s32[128,16384]{1,0:T(8,128)}, u32[]{:S(2)}) copy-start(s32[128,16384]{1,0:T(8,128)} %photons.1) | copy-start | bytes 25165828
  4.0 0.9 %copy-start.1 = (f32[65536]{0:T(1024)S(1)}, f32[65536]{0:T(1024)}, u32[]{:S(2)}) copy-start(f32[65536]{0:T(1024)} %param.9) | copy-start | bytes 786436
  5.0 0.7 %copy-start.2 = (s32[128,4,8]{0,2,1:T(8,128)S(1)}, s32[128,4,8]{0,2,1:T(8,128)}, u32[]{:S(2)}) copy-start(s32[128,4,8]{0,2,1:T(8,128)} %param.7) | copy-start | bytes 49156
  5.7 0.7 %copy-start.3 = (s32[4,512]{1,0:T(4,128)S(1)}, s32[4,512]{1,0:T(4,128)}, u32[]{:S(2)}) copy-start(s32[4,512]{1,0:T(4,128)} %maps.1) | copy-start | bytes 24580
  6.4 0.7 %copy-start.4 = (f32[128]{0:T(128)S(1)}, f32[128]{0:T(128)}, u32[]{:S(2)}) copy-start(f32[128]{0:T(128)} %param.10) | copy-start | bytes 1540
  7.0 0.7 %copy-start.5 = (f32[8]{0:T(128)S(1)}, f32[8]{0:T(128)}, u32[]{:S(2)}) copy-start(f32[8]{0:T(128)} %param.11) | copy-start | bytes 100

commit v2 on v1

--- a/solution.py
+++ b/solution.py
@@ -129,10 +129,13 @@
         return c
 
     rows = jnp.zeros((D, 128), jnp.int32)
-    half = F // 2
-    for i in range(half):
+    for i in range(F):
         rows = sums(i, rows)
-        send_cols(i)
+        if i < F - 1:
+            send_cols(i)
+
+    note[0, 1:2, :] = jnp.sum(rows.astype(jnp.float32).T, axis=0, keepdims=True)
+    parts[f] = cols[F - 1]
 
     own_map.wait()
     maps_in = all_of(map_v, map_sem, O - 1)
@@ -173,13 +176,6 @@
 
     expected = expected_of([stat[g, OL + 1:OL + 2, :] for g in range(F)])
 
-    for i in range(half, F):
-        rows = sums(i, rows)
-        if i < F - 1:
-            send_cols(i)
-
-    note[0, 1:2, :] = jnp.sum(rows.astype(jnp.float32).T, axis=0, keepdims=True)
-    parts[f] = cols[F - 1]
     parts_in = all_of(parts, col_sem, F - 1)
     parts_in.wait_recv()
     pixel = parts[0]
@@ -261,9 +257,9 @@
     hbm = pl.BlockSpec(memory_space=pltpu.HBM)
     gain, phi = pl.pallas_call(
         body,
-        out_shape=(jax.ShapeDtypeStruct((F, NB, BLOCK), f32), jax.ShapeDtypeStruct((1, D), f32)),
+        out_shape=(pltpu.VMEM((F, NB, BLOCK), f32), pltpu.VMEM((1, D), f32)),
         in_specs=[hbm] * 6,
-        out_specs=(hbm, hbm),
+        out_specs=(pl.BlockSpec(memory_space=pltpu.VMEM),)*2,
         scratch_shapes=[
             V((F, CH, D, NB * BLOCK // CH), i32),
             V((OL, L, D), i32), V((1, D), f32), V((1, L), f32),
@@ -275,7 +271,7 @@
             dma((F, CH)), dma((5,)), dma((2,)), dma((3,)), dma((2,)), dma((2,)), dma((ITERS, 2)), dma((2,)),
         ],
         compiler_params=pltpu.CompilerParams(
-            collective_id=0, has_side_effects=True, vmem_limit_bytes=40 * 1024 * 1024),
+            collective_id=0, has_side_effects=True, vmem_limit_bytes=63 * 1024 * 1024),
     )(photons, jnp.transpose(masses, (1, 2, 0)), maps, model.reshape(MB, BLOCK),
       fluence.reshape(1, D), level_scale.reshape(1, L))
     return gain.reshape(-1), phi.reshape(-1)

time: 32.1 us -> 22.5 us (0.70)
  local copies, waits for them, and re-layouts: 8.19 us -> 1.15 us
  Pallas kernels: 23 us -> 20.5 us
    unnamed x14 -> x2, local copies, waits for them, and re-layouts: 8.19 us -> 1.15 us
    pallas_call x1, Pallas kernels: 23 us -> 20.5 us  [on_device(): pl.pallas_call(body, out_shape=(pltpu.VMEM((F, NB, BLOCK), f32), pltpu.VM...]
where the time goes in v2:
time: 22.5 us; the launch traced here: 22.3 us
  Pallas kernels  20.5 us (91%)
  local copies, waits for them, and re-layouts  1.15 us (5%)
  between operations  0.64 us (3%)
    pallas_call x1, Pallas kernels, on_device(): pl.pallas_call(body, out_shape=(pltpu.VMEM((F, NB, BLOCK), f32), pltpu.VM...  20.5 us
    unnamed x2, local copies, waits for them, and re-layouts  1.15 us

profile of v2, /device:TPU:0, one launch (start us, length us, event | category | flops | bytes accessed | tf_op | source)
XLA Modules:
  0.0 22.3 jit_solution(6725891869195338314)
XLA Ops:
  0.6 20.5 %shard_map.77 = (f32[4,32,128]{2,1,0:T(8,128)S(1)}, f32[1,128]{1,0:T(1,128)S(1)}) custom-call(s32[128,16384]{1,0:T(8,128)} %photons.1, s32[4,8,128]{2,1,0:T(8,128)} %bitcast.9, s32[4,512]{1,0:T(4,128)} %maps.1, f32[512,128]{1,0:T(8,128)} %bitcast.8, f32[1,128]{1,0:T(1,128)} %bitcast.10, f32[1,8]{1,0:T(1,128)} %bitcast.11), custom_call_target="tpu_custom_call" | custom-call | tf_op jit(solution)/shard_map/pallas_call | solution.py:258
  21.1 0.6 %copy.10 = f32[16384]{0:T(1024)} copy(f32[16384]{0:T(1024)S(1)} %bitcast.6) | data formatting | bytes 131072
  21.8 0.5 %copy.11 = f32[128]{0:T(128)} copy(f32[128]{0:T(128)S(1)} %bitcast.7) | data formatting | bytes 1024

commit v3 on v2

--- a/solution.py
+++ b/solution.py
@@ -26,6 +26,7 @@
     me = o * F + f
     width = NB * BLOCK
     piece = width // CH
+    U = 8 if piece % 1024 == 0 else 1
 
     def spot(t):
         n = lax.rem(me + t, N)
@@ -109,11 +110,19 @@
         for c in range(CH):
             read(i, c).wait()
 
-            def tile(q, acc):
-                x = ph[i, c, :, pl.ds(pl.multiple_of(q * 128, 128), 128)]
-                cols[i, pl.ds(c * (piece // 128) + q, 1), :] = jnp.sum(x, axis=0, keepdims=True).astype(jnp.float32)
-                return acc + x
-            rows = lax.fori_loop(0, piece // 128, tile, rows, unroll=2)
+            def tiles(q, acc):
+                out = []
+                for u in range(U):
+                    x = ph[i, c, :, pl.ds(pl.multiple_of((q * U + u) * 128, 128), 128)].reshape(D // 8, 8, 128)
+                    col = x[0]
+                    for d in range(1, D // 8):
+                        col += x[d]
+                    out.append(jnp.sum(col, axis=0, keepdims=True))
+                    acc += x.reshape(D, 128)
+                here = pl.multiple_of(c * (piece // 128) + q * U, U)
+                cols[i, pl.ds(here, U), :] = jnp.concatenate(out, axis=0).astype(jnp.float32)
+                return acc
+            rows = lax.fori_loop(0, piece // 128 // U, tiles, rows)
         return rows
 
     def send_cols(i):
@@ -159,8 +168,9 @@
 
     def look(r, carry):
         a, k = lax.div(r, OL), lax.rem(r, OL)
+        got = [table[pl.ds(map_s[a, k, base + b], 1), :] for b in range(NB)]
         for b in range(NB):
-            sl[r, b:b + 1, :] = table[pl.ds(map_s[a, k, base + b], 1), :]
+            sl[r, b:b + 1, :] = got[b]
         return carry
     lax.fori_loop(0, R, look, 0)
 
@@ -247,7 +257,7 @@
     MB = maps.shape[1]
     N = O * F
     NB = wide // F // BLOCK
-    CH = 2 if NB % 2 == 0 else 1
+    CH = 1
     R = O * OL
     f32, i32 = jnp.float32, jnp.int32
     V = pltpu.VMEM

time: 22.5 us -> 21.6 us (0.960)
  Pallas kernels: 20.5 us -> 19.6 us
    pallas_call x1, Pallas kernels: 20.5 us -> 19.6 us  [on_device(): pl.pallas_call(body, out_shape=(pltpu.VMEM((F, NB, BLOCK), f32), pltpu.VM...]
where the time goes in v3:
time: 21.6 us; the launch traced here: 21.3 us
  Pallas kernels  19.6 us (91%)
  local copies, waits for them, and re-layouts  1.15 us (5%)
  between operations  0.64 us (3%)
    pallas_call x1, Pallas kernels, on_device(): pl.pallas_call(body, out_shape=(pltpu.VMEM((F, NB, BLOCK), f32), pltpu.VM...  19.6 us
    unnamed x2, local copies, waits for them, and re-layouts  1.15 us

profile of v3, /device:TPU:0, one launch (start us, length us, event | category | flops | bytes accessed | tf_op | source)
XLA Modules:
  0.0 21.3 jit_solution(15250091214310240809)
XLA Ops:
  0.6 19.6 %shard_map.77 = (f32[4,32,128]{2,1,0:T(8,128)S(1)}, f32[1,128]{1,0:T(1,128)S(1)}) custom-call(s32[128,16384]{1,0:T(8,128)} %photons.1, s32[4,8,128]{2,1,0:T(8,128)} %bitcast.9, s32[4,512]{1,0:T(4,128)} %maps.1, f32[512,128]{1,0:T(8,128)} %bitcast.8, f32[1,128]{1,0:T(1,128)} %bitcast.10, f32[1,8]{1,0:T(1,128)} %bitcast.11), custom_call_target="tpu_custom_call" | custom-call | tf_op jit(solution)/shard_map/pallas_call | solution.py:268
  20.2 0.6 %copy.10 = f32[16384]{0:T(1024)} copy(f32[16384]{0:T(1024)S(1)} %bitcast.6) | data formatting | bytes 131072
  20.8 0.5 %copy.11 = f32[128]{0:T(128)} copy(f32[128]{0:T(128)S(1)} %bitcast.7) | data formatting | bytes 1024
